TPU v7x, 512 devices: a whole 4x4x16 slice. The times are simulated.
512 devices in a mesh: grp: 64 (over x, z), dev: 8 (over y, core).
Axes of the slice: x: 4, y: 4, z: 16, core: 2. Of those that a mesh axis runs over, the one named last changes fastest.
Arguments:
- tokens: bfloat16 [32768, 768], P(('grp', 'dev')), may hold values from -6 to 6
- expert_ids: int32 [32768, 8], P(('grp', 'dev')), may hold values from 0 to 511, as said below
- gates: bfloat16 [32768, 8], P(('grp', 'dev')), may hold values from 0.099609375 to 0.5
- w_in: bfloat16 [512, 768, 1536], P(('grp', 'dev')), may hold values from -0.21875 to 0.21875
- w_out: bfloat16 [512, 1536, 768], P(('grp', 'dev')), may hold values from -0.15625 to 0.15625
Outputs:
- mixed: bfloat16 [32768, 768], P(('grp', 'dev'))
Inputs may be any that keep to these rules, and one draw needn't show every extreme that they name: `expert_ids`: row t lists 8 experts; columns 2 * k and 2 * k + 1 are two different experts of one group (experts g * 8 to g * 8 + 7 form group g), and the four groups of a row differ. The owner of token t is t // 64, and its dev index is the owner modulo 8. The tokens of one owner pick one group at most 12 times, and every owner reaches it for some group. The tokens whose owners share a dev index pick each group exactly 4 * 64 times in all and each expert at most 192 times; in every group one expert is picked 192 times by the tokens of every dev index.
All inputs are finite; a program needn't handle non-finite values.
Results may differ from a plain program's by a relative error of at most 0.0057.
Values may be sent and summed in bfloat16 or wider, within the bound.
A program may use at most 64 MiB of HBM per device.

v0:
```python
import jax
import jax.numpy as jnp
from jax import lax
from jax.sharding import PartitionSpec as P


def earlier_count(onehot):
    return jnp.cumsum(onehot, axis=0) - onehot


def contract_rows(left, right):
    return lax.dot_general(
        left,
        right,
        (((0,), (0,)), ((), ())),
        precision=lax.Precision.HIGHEST,
        preferred_element_type=jnp.float32,
    )


def expert_rows(slot_block, w_first, w_second):

    def one_block(rows_block):
        hidden = jnp.maximum(
            jnp.dot(rows_block, w_first, preferred_element_type=jnp.float32), 0.0
        ).astype(jnp.bfloat16)
        return jnp.dot(hidden, w_second, preferred_element_type=jnp.float32).astype(jnp.bfloat16)

    return lax.map(one_block, slot_block)


def seat_sources(seat_of, valid, seat_total):
    item_count = seat_of.shape[0]
    target_seat = jnp.where(valid, seat_of, seat_total)
    empty_seats = jnp.full((seat_total,), item_count, jnp.int32)
    return empty_seats.at[target_seat].set(jnp.arange(item_count, dtype=jnp.int32), mode="drop")


def per_device(tokens, expert_ids, gates, w_in, w_out):
    n_grp = lax.axis_size("grp")
    n_dev = lax.axis_size("dev")
    token_count, feature_width = tokens.shape
    cap_grp = min(token_count, 3 * ((4 * token_count + n_grp - 1) // n_grp))
    cap_exp = min(4 * token_count, 24 * token_count // n_dev)
    seat_total = n_dev * cap_exp
    zero_half = jnp.zeros((), jnp.bfloat16)
    w_first = w_in[0]
    w_second = w_out[0]
    pair_ids = expert_ids.reshape(token_count * 4, 2)
    pair_group = pair_ids[:, 0] // n_dev
    group_hot = (pair_group[:, None] == jnp.arange(n_grp)[None, :]).astype(jnp.int32)
    group_rank = jnp.sum(earlier_count(group_hot) * group_hot, axis=1)
    target = pair_group * cap_grp + group_rank
    slot_count = n_grp * cap_grp
    placed = (target[None, :] == jnp.arange(slot_count)[:, None]).astype(jnp.int32)
    token_hot = placed.reshape(slot_count, token_count, 4).sum(axis=2)
    rows_out = jnp.dot(
        token_hot.astype(jnp.bfloat16), tokens, preferred_element_type=jnp.float32
    ).astype(jnp.bfloat16)
    local_ids = pair_ids % n_dev
    picks_out = jnp.dot(placed, local_ids + 1) - 1
    gains_out = jnp.dot(
        placed.astype(jnp.bfloat16),
        gates.reshape(token_count * 4, 2),
        preferred_element_type=jnp.float32,
    ).astype(jnp.bfloat16)
    rows_in, picks_in, gains_in = (
        lax.all_to_all(
            rows_out.reshape(n_grp, cap_grp, feature_width),
            "grp",
            split_axis=0,
            concat_axis=0,
            tiled=True,
        ),
        lax.all_to_all(
            picks_out.reshape(n_grp, cap_grp, 2), "grp", split_axis=0, concat_axis=0, tiled=True
        ),
        lax.all_to_all(
            gains_out.reshape(n_grp, cap_grp, 2), "grp", split_axis=0, concat_axis=0, tiled=True
        ),
    )
    relay_rows = rows_in.reshape(slot_count, feature_width)
    relay_picks = picks_in.reshape(slot_count, 2)
    relay_gains = gains_in.reshape(slot_count, 2)
    live_count = 4 * token_count
    slot_live = (relay_picks[:, 0] >= 0).astype(jnp.int32)
    slot_order = jnp.cumsum(slot_live) - 1
    packed = (
        (slot_order[None, :] == jnp.arange(live_count)[:, None]) & (slot_live[None, :] > 0)
    ).astype(jnp.int32)
    packed_rows = jnp.dot(
        packed.astype(jnp.bfloat16), relay_rows, preferred_element_type=jnp.float32
    ).astype(jnp.bfloat16)
    packed_picks = jnp.dot(packed, relay_picks)
    packed_gains = jnp.dot(
        packed.astype(jnp.bfloat16), relay_gains, preferred_element_type=jnp.float32
    ).astype(jnp.bfloat16)
    group_rows, group_picks, group_gains = (
        lax.all_gather(packed_rows, "dev", axis=0, tiled=True),
        lax.all_gather(packed_picks, "dev", axis=0, tiled=True),
        lax.all_gather(packed_gains, "dev", axis=0, tiled=True),
    )
    gathered_count = group_rows.shape[0]
    chosen = jnp.sum((group_picks == lax.axis_index("dev")).astype(jnp.int32), axis=1)
    expert_seat = jnp.cumsum(chosen) - 1
    seat_source = seat_sources(expert_seat, chosen > 0, seat_total)
    seat_live = seat_source < gathered_count
    taken_rows = jnp.take(group_rows, jnp.minimum(seat_source, gathered_count - 1), axis=0)
    expert_in = jnp.where(seat_live[:, None], taken_rows, zero_half)
    expert_out = expert_rows(
        expert_in.reshape(n_dev, cap_exp, feature_width), w_first, w_second
    ).reshape(seat_total, feature_width)
    spread_rows = jnp.take(expert_out, jnp.clip(expert_seat, 0, seat_total - 1), axis=0)
    spread = jnp.where((chosen > 0)[:, None], spread_rows, zero_half)
    back = lax.all_to_all(
        spread.reshape(n_dev, live_count, feature_width),
        "dev",
        split_axis=0,
        concat_axis=0,
        tiled=True,
    )
    match = (packed_picks[None, :, :] == jnp.arange(n_dev)[:, None, None]).astype(jnp.float32)
    row_weights = jnp.sum(match * packed_gains.astype(jnp.float32)[None, :, :], axis=2)
    packed_sum = jnp.sum(row_weights[:, :, None] * back.astype(jnp.float32), axis=0)
    partial_value = contract_rows(packed.astype(jnp.float32), packed_sum)
    returned_sums = lax.all_to_all(
        partial_value.reshape(n_grp, cap_grp, feature_width),
        "grp",
        split_axis=0,
        concat_axis=0,
        tiled=True,
    )
    mixed = contract_rows(
        token_hot.astype(jnp.float32), returned_sums.reshape(slot_count, feature_width)
    )
    return mixed.astype(jnp.bfloat16)


def solution(mesh):
    return jax.shard_map(
        per_device,
        mesh=mesh,
        in_specs=(
            P(("grp", "dev"), None),
            P(("grp", "dev"), None),
            P(("grp", "dev"), None),
            P(("grp", "dev"), None, None),
            P(("grp", "dev"), None, None),
        ),
        out_specs=P(("grp", "dev"), None),
        check_vma=False,
    )
```

profile of v0, /device:TPU:6, one launch (start us, length us, event | category | flops | bytes accessed | tf_op | source)
XLA Modules:
  0.0 426.4 jit_solution(9296313556347692572)
XLA Ops:
  6.5 0.8 copy.40
  7.3 0.1 reshape.290
  7.4 0.2 slice_reduce_fusion
  7.6 0.6 reduce-window.24
  8.2 0.2 slice_reduce_fusion.1
  8.5 0.1 fusion.44
  8.6 0.6 convolution_add_fusion
  9.2 0.1 reshape.292
  9.3 0.7 copy.43
  10.0 18.8 %all-to-all-start = ((s32[64,12,2]{1,2,0:T(2,128)}), s32[64,12,2]{1,2,0:T(2,128)S(1)}, u32[]{:S(2)}, u32[]{:S(2)}) async-start(s32[64,12,2]{1,2,0:T(2,128)} %copy.43), calls=%async_computation | async-start | bytes 131072 | tf_op jit(solution)/shard_map/all_to_all | solution.py:75
  28.8 0.1 squeeze.16
  28.9 0.1 reduce_sum.48
  29.1 0.2 convert_reduce_fusion
  29.3 0.5 convolution_convert_fusion.1
  29.8 1.3 reshape.303
  31.1 10.6 %all-to-all-done = s32[64,12,2]{1,2,0:T(2,128)S(1)} async-done(((s32[64,12,2]{1,2,0:T(2,128)}), s32[64,12,2]{1,2,0:T(2,128)S(1)}, u32[]{:S(2)}, u32[]{:S(2)}) %all-to-all-start) | async-done | bytes 6176 | tf_op jit(solution)/shard_map/all_to_all | solution.py:75
  41.7 6.4 %all-to-all-start.2 = ((bf16[64,12,768]{2,1,0:T(8,128)(2,1)}), bf16[64,12,768]{2,1,0:T(8,128)(2,1)S(1)}, u32[]{:S(2)}, u32[]{:S(2)}) async-start(bf16[64,12,768]{2,1,0:T(8,128)(2,1)} %reshape.303), calls=%async_computation.2 | async-start | bytes 3145728 | tf_op jit(solution)/shard_map/all_to_all | solution.py:68
  48.2 0.1 reshape.293
  48.3 0.3 reduce-window.26
  48.7 0.1 slice_reduce_fusion.3
  48.9 74.3 %all-to-all-done.2 = bf16[64,12,768]{2,1,0:T(8,128)(2,1)S(1)} async-done(((bf16[64,12,768]{2,1,0:T(8,128)(2,1)}), bf16[64,12,768]{2,1,0:T(8,128)(2,1)S(1)}, u32[]{:S(2)}, u32[]{:S(2)}) %all-to-all-start.2) | async-done | bytes 1179680 | tf_op jit(solution)/shard_map/all_to_all | solution.py:68
  123.2 0.3 reshape.304
  123.5 1.3 convolution_convert_fusion.2
  124.8 0.1 copy.47
  124.9 0.1 reshape.295
  125.0 0.2 convolution_convert_fusion.4
  125.2 0.1 reshape.296
  125.4 0.6 copy.48
  126.0 6.9 %all-to-all-start.1 = ((bf16[64,12,2]{1,2,0:T(2,128)(2,1)}), bf16[64,12,2]{1,2,0:T(2,128)(2,1)S(1)}, u32[]{:S(2)}, u32[]{:S(2)}) async-start(bf16[64,12,2]{1,2,0:T(2,128)(2,1)} %copy.48), calls=%async_computation.1 | async-start | bytes 65536 | tf_op jit(solution)/shard_map/all_to_all | solution.py:78
  132.9 0.6 fusion.19
  133.5 12.1 %all_gather.6 = s32[2048,2]{0,1:T(2,128)S(1)} all-gather(s32[256,2]{0,1:T(2,128)S(1)} %fusion.19), channel_id=1, replica_groups=mesh['grp'=64,'dev'=8] {'dev'}, dimensions={0}, use_global_device_ids=true | all-gather | bytes 18432 | tf_op jit(solution)/shard_map/all_gather | solution.py:100
  145.6 0.3 reduce-window.36
  146.0 0.1 slice_reduce_fusion.2
  146.2 0.1 reshape.300
  146.2 0.1 copy.50
  146.4 8.0 %scatter_custom_fusion = s32[1536]{0:T(1024)S(1)} fusion(s32[2048]{0:T(1024)S(1)} %bitcast.90, s32[2048]{0:T(1024)S(1)} %iota.29, s32[]{:T(128)} %constant.103.clone.1), kind=kCustom, calls=%fused_computation.109 | custom fusion | bytes 6148 | tf_op jit(solution)/shard_map/scatter | solution.py:36
  154.5 0.1 broadcast_in_dim.74
  154.6 0.1 broadcast_in_dim.76
  154.8 9.0 %gather_fusion = bf16[1536,768]{1,0:T(8,128)(2,1)} fusion(bf16[2048,768]{1,0:T(8,128)(2,1)} %all-gather.2.cloned.1.call-done, s32[2048]{0:T(1024)S(1)} %pad_clamp_fusion), kind=kCustom, calls=%fused_computation | custom fusion | bytes 4724736 | tf_op jit(solution)/shard_map/jit(_take)/gather | solution.py:108
  163.8 3.0 select_select_fusion.1
  166.8 29.7 %while.11 = (s32[]{:T(128)}, bf16[8,192,768]{2,1,0:T(8,128)(2,1)S(1)}, bf16[8,192,768]{2,1,0:T(8,128)(2,1)}, bf16[768,1536]{1,0:T(8,128)(2,1)}, bf16[1536,768]{1,0:T(8,128)(2,1)}) while((s32[]{:T(128)}, bf16[8,192,768]{2,1,0:T(8,128)(2,1)S(1)}, bf16[8,192,768]{2,1,0:T(8,128)(2,1)}, bf16[768,1536]{1,0:T(8,128)(2,1)}, ...), condition=%wide.region_12.13_spmd.clone, body=%wide.region_11.12_spmd.sunk.clone | while | flops 906706944 | bytes 5309509 | solution.py:29
  166.8 3.7 fusion.84
  170.5 3.7 fusion.84
  174.2 3.7 fusion.84
  177.9 3.7 fusion.84
  181.7 3.7 fusion.84
  185.4 3.7 fusion.84
  189.1 3.7 fusion.84
  192.8 3.7 fusion.84
  196.5 9.4 %gather_fusion.1 = bf16[2048,768]{1,0:T(8,128)(2,1)} fusion(bf16[1536,768]{1,0:T(8,128)(2,1)S(1)} %bitcast.82, s32[2048]{0:T(1024)S(1)} %broadcast_clamp_fusion), kind=kCustom, calls=%fused_computation.1 | custom fusion | bytes 6299648 | tf_op jit(solution)/shard_map/jit(_take)/gather | solution.py:113
  205.9 3.5 select_select_fusion
  209.3 3.8 all-to-all-start.3
  213.2 0.1 reshape.297
  213.3 0.1 gt.37
  213.4 0.1 copy.46
  213.6 0.1 sub.39
  213.8 0.2 fusion.11
  214.0 37.3 %all-to-all-done.3 = bf16[8,256,768]{2,1,0:T(8,128)(2,1)S(1)} async-done(((bf16[8,256,768]{2,1,0:T(8,128)(2,1)}), bf16[8,256,768]{2,1,0:T(8,128)(2,1)S(1)}, u32[]{:S(2)}, u32[]{:S(2)}) %all-to-all-start.3) | async-done | bytes 3145760 | tf_op jit(solution)/shard_map/all_to_all | solution.py:115
  251.4 0.6 multiply_reduce_fusion
  252.0 2.2 fusion.12
  254.2 1.4 copy.51
  255.7 158.5 %all_to_all.25 = f32[64,12,768]{2,1,0:T(8,128)S(1)} all-to-all(f32[64,12,768]{2,1,0:T(8,128)S(1)} %copy.51), channel_id=1, replica_groups=mesh['grp'=64,'dev'=8] {'grp'}, dimensions={0} | all-to-all | bytes 4718592 | tf_op jit(solution)/shard_map/all_to_all | solution.py:126
  414.2 1.5 reshape.306
  415.7 3.9 convolution_convert_fusion.3
  (39 shorter events, 1.0 us)
Async XLA Ops:
  6.5 22.8 %copy-start = (bf16[64,768]{1,0:T(8,128)(2,1)S(1)}, bf16[64,768]{1,0:T(8,128)(2,1)}, u32[]{:S(2)}) copy-start(bf16[64,768]{1,0:T(8,128)(2,1)} %param.7) | copy-start | bytes 294916
  10.0 31.7 %all-to-all-start = ((s32[64,12,2]{1,2,0:T(2,128)}), s32[64,12,2]{1,2,0:T(2,128)S(1)}, u32[]{:S(2)}, u32[]{:S(2)}) async-start(s32[64,12,2]{1,2,0:T(2,128)} %copy.43), calls=%async_computation | async-start | bytes 131072 | tf_op jit(solution)/shard_map/all_to_all | solution.py:75
  41.7 81.5 %all-to-all-start.2 = ((bf16[64,12,768]{2,1,0:T(8,128)(2,1)}), bf16[64,12,768]{2,1,0:T(8,128)(2,1)S(1)}, u32[]{:S(2)}, u32[]{:S(2)}) async-start(bf16[64,12,768]{2,1,0:T(8,128)(2,1)} %reshape.303), calls=%async_computation.2 | async-start | bytes 3145728 | tf_op jit(solution)/shard_map/all_to_all | solution.py:68
  48.2 106.7 %all-gather.2.cloned.1.call-start = ((), (), s32[]{:S(2)}) async-start(), calls=%async_computation.5 | async-start | bytes 3538944 | tf_op jit(solution)/shard_map/all_gather | solution.py:99
  48.9 75.8 %copy-start.1 = (bf16[64,8]{0,1:T(8,128)(2,1)S(1)}, bf16[64,8]{0,1:T(8,128)(2,1)}, u32[]{:S(2)}) copy-start(bf16[64,8]{0,1:T(8,128)(2,1)} %param.9) | copy-start | bytes 3076
  126.0 83.3 %all-to-all-start.1 = ((bf16[64,12,2]{1,2,0:T(2,128)(2,1)}), bf16[64,12,2]{1,2,0:T(2,128)(2,1)S(1)}, u32[]{:S(2)}, u32[]{:S(2)}) async-start(bf16[64,12,2]{1,2,0:T(2,128)(2,1)} %copy.48), calls=%async_computation.1 | async-start | bytes 65536 | tf_op jit(solution)/shard_map/all_to_all | solution.py:78
  209.3 42.0 %all-to-all-start.3 = ((bf16[8,256,768]{2,1,0:T(8,128)(2,1)}), bf16[8,256,768]{2,1,0:T(8,128)(2,1)S(1)}, u32[]{:S(2)}, u32[]{:S(2)}) async-start(bf16[8,256,768]{2,1,0:T(8,128)(2,1)} %select_select_fusion), calls=%async_computation.3 | async-start | bytes 6291456 | tf_op jit(solution)/shard_map/all_to_all | solution.py:115
Sparse Core Ops, SparseCore 0:
  124.9 28.0 all-gather.1
where the time goes:
time: 427 us; the launch traced here: 426 us
  blocking collectives  171 us (40%)
  waiting for transfers between devices  122 us (29%)
  matrix products  38.9 us (9%)
  starting transfers between devices  36 us (8%)
  local copies, waits for them, and re-layouts  35.5 us (8%)
  between operations  13.7 us (3%)
  other arithmetic  9.29 us (2%)
    all_to_all x1, blocking collectives, per_device(): lax.all_to_all(partial_value.reshape(n_grp, cap_grp, feature_width), 'grp...  159 us
    all_to_all x1, waiting for transfers between devices, per_device(): lax.all_to_all(rows_out.reshape(n_grp, cap_grp, feature_width), 'grp', sp...  74.3 us
    all_to_all x1, waiting for transfers between devices, per_device(): lax.all_to_all(spread.reshape(n_dev, live_count, feature_width), 'dev', s...  37.3 us
    dot_general x8, matrix products, one_block(): jnp.dot(hidden, w_second, preferred_element_type=jnp.float32)  29.5 us
    all_to_all x1, starting transfers between devices, per_device(): lax.all_to_all(picks_out.reshape(n_grp, cap_grp, 2), 'grp', split_axis=0,...  18.8 us
    all_gather x1, blocking collectives, per_device(): lax.all_gather(packed_picks, 'dev', axis=0, tiled=True)  12.1 us
    all_to_all x1, waiting for transfers between devices, per_device(): lax.all_to_all(picks_out.reshape(n_grp, cap_grp, 2), 'grp', split_axis=0,...  10.6 us
    gather x1, local copies, waits for them, and re-layouts, per_device(): jnp.take(expert_out, jnp.clip(expert_seat, 0, seat_total - 1), axis=0)  9.38 us
  transfers between devices with their start and end apart: 5, of which 3 were waited for; matrix products, arithmetic and copies ran while one was open for 16% of the time, Pallas kernels for 0%

commit v1 on v0

--- a/solution.py
+++ b/solution.py
@@ -2,6 +2,18 @@
 import jax.numpy as jnp
 from jax import lax
 from jax.sharding import PartitionSpec as P
+
+
+def collect(array, axis, dim):
+    ways, here, step = (lax.axis_size(axis), lax.axis_index(axis), array.shape[dim])
+    line, have = (array, 1)
+    while have < ways:
+        line = jnp.concatenate(
+            [line, lax.ppermute(line, axis, [(d, (d - have) % ways) for d in range(ways)])],
+            axis=dim,
+        )
+        have = 2 * have
+    return jnp.roll(line, here * step, axis=dim)
 
 
 def earlier_count(onehot):
@@ -97,7 +109,7 @@
     ).astype(jnp.bfloat16)
     group_rows, group_picks, group_gains = (
         lax.all_gather(packed_rows, "dev", axis=0, tiled=True),
-        lax.all_gather(packed_picks, "dev", axis=0, tiled=True),
+        collect(packed_picks, "dev", 0),
         lax.all_gather(packed_gains, "dev", axis=0, tiled=True),
     )
     gathered_count = group_rows.shape[0]

time: 427 us -> 430 us (level)
  blocking collectives: 171 us -> 159 us
  starting transfers between devices: 36 us -> 43.8 us
  waiting for transfers between devices: 122 us -> 129 us
    all_gather x1 -> x0, blocking collectives: 12.1 us -> none  [per_device(): lax.all_gather(packed_picks, 'dev', axis=0, tiled=True)]
    ppermute x0 -> x3, waiting for transfers between devices: none -> 7.03 us  [collect(): lax.ppermute(line, axis, [(d, (d - have) % ways) for d in range(ways)])]
    ppermute x0 -> x3, starting transfers between devices: none -> 5.68 us  [collect(): lax.ppermute(line, axis, [(d, (d - have) % ways) for d in range(ways)])]
  transfers between devices with their start and end apart: 5 -> 8, of which waited for: 3 -> 5; matrix products, arithmetic and copies ran while one was open for 16% -> 16% of each run, Pallas kernels for 0% -> 0%
where the time goes in v1:
time: 430 us; the launch traced here: 429 us
  blocking collectives  159 us (37%)
  waiting for transfers between devices  129 us (30%)
  starting transfers between devices  43.8 us (10%)
  matrix products  39 us (9%)
  local copies, waits for them, and re-layouts  35.5 us (8%)
  between operations  13.8 us (3%)
  other arithmetic  9.31 us (2%)
    all_to_all x1, blocking collectives, per_device(): lax.all_to_all(partial_value.reshape(n_grp, cap_grp, feature_width), 'grp...  159 us
    all_to_all x1, waiting for transfers between devices, per_device(): lax.all_to_all(rows_out.reshape(n_grp, cap_grp, feature_width), 'grp', sp...  74.3 us
    all_to_all x1, waiting for transfers between devices, per_device(): lax.all_to_all(spread.reshape(n_dev, live_count, feature_width), 'dev', s...  37.3 us
    dot_general x8, matrix products, one_block(): jnp.dot(hidden, w_second, preferred_element_type=jnp.float32)  29.5 us
    all_to_all x1, starting transfers between devices, per_device(): lax.all_to_all(picks_out.reshape(n_grp, cap_grp, 2), 'grp', split_axis=0,...  18.8 us
    all_to_all x1, waiting for transfers between devices, per_device(): lax.all_to_all(picks_out.reshape(n_grp, cap_grp, 2), 'grp', split_axis=0,...  10.6 us
    gather x1, local copies, waits for them, and re-layouts, per_device(): jnp.take(expert_out, jnp.clip(expert_seat, 0, seat_total - 1), axis=0)  9.38 us
    all_to_all x1, starting transfers between devices, per_device(): lax.all_to_all(gains_out.reshape(n_grp, cap_grp, 2), 'grp', split_axis=0,...  9.05 us
  transfers between devices with their start and end apart: 8, of which 5 were waited for; matrix products, arithmetic and copies ran while one was open for 16% of the time, Pallas kernels for 0%

profile of v1, /device:TPU:6, one launch (start us, length us, event | category | flops | bytes accessed | tf_op | source)
XLA Modules:
  0.0 429.3 jit_solution(7352874285917221596)
XLA Ops:
  6.5 0.8 copy.40
  7.4 0.2 slice_reduce_fusion
  7.6 0.6 reduce-window.24
  8.2 0.2 slice_reduce_fusion.1
  8.5 0.1 fusion.44
  8.6 0.6 convolution_add_fusion
  9.2 0.1 reshape.292
  9.3 0.7 copy.43
  10.0 18.8 %all-to-all-start = ((s32[64,12,2]{1,2,0:T(2,128)}), s32[64,12,2]{1,2,0:T(2,128)S(1)}, u32[]{:S(2)}, u32[]{:S(2)}) async-start(s32[64,12,2]{1,2,0:T(2,128)} %copy.43), calls=%async_computation | async-start | bytes 131072 | tf_op jit(solution)/shard_map/all_to_all | solution.py:87
  28.8 0.1 squeeze.16
  28.9 0.1 reduce_sum.48
  29.1 0.2 convert_reduce_fusion
  29.3 0.5 convolution_convert_fusion.1
  29.8 1.3 reshape.303
  31.1 10.6 %all-to-all-done = s32[64,12,2]{1,2,0:T(2,128)S(1)} async-done(((s32[64,12,2]{1,2,0:T(2,128)}), s32[64,12,2]{1,2,0:T(2,128)S(1)}, u32[]{:S(2)}, u32[]{:S(2)}) %all-to-all-start) | async-done | bytes 6176 | tf_op jit(solution)/shard_map/all_to_all | solution.py:87
  41.7 6.4 %all-to-all-start.2 = ((bf16[64,12,768]{2,1,0:T(8,128)(2,1)}), bf16[64,12,768]{2,1,0:T(8,128)(2,1)S(1)}, u32[]{:S(2)}, u32[]{:S(2)}) async-start(bf16[64,12,768]{2,1,0:T(8,128)(2,1)} %reshape.303), calls=%async_computation.2 | async-start | bytes 3145728 | tf_op jit(solution)/shard_map/all_to_all | solution.py:80
  48.2 0.1 reshape.293
  48.3 0.3 reduce-window.26
  48.7 0.1 slice_reduce_fusion.3
  48.9 74.3 %all-to-all-done.2 = bf16[64,12,768]{2,1,0:T(8,128)(2,1)S(1)} async-done(((bf16[64,12,768]{2,1,0:T(8,128)(2,1)}), bf16[64,12,768]{2,1,0:T(8,128)(2,1)S(1)}, u32[]{:S(2)}, u32[]{:S(2)}) %all-to-all-start.2) | async-done | bytes 1179680 | tf_op jit(solution)/shard_map/all_to_all | solution.py:80
  123.2 0.3 reshape.304
  123.5 1.3 convolution_convert_fusion.2
  124.8 0.1 copy.47
  124.9 0.1 reshape.295
  125.0 0.6 constant_dynamic-update-slice_fusion.7
  125.5 0.2 convolution_convert_fusion.4
  125.8 0.1 reshape.296
  125.9 0.6 copy.48
  126.6 9.0 %all-to-all-start.1 = ((bf16[64,12,2]{1,2,0:T(2,128)(2,1)}), bf16[64,12,2]{1,2,0:T(2,128)(2,1)S(1)}, u32[]{:S(2)}, u32[]{:S(2)}) async-start(bf16[64,12,2]{1,2,0:T(2,128)(2,1)} %copy.48), calls=%async_computation.1 | async-start | bytes 65536 | tf_op jit(solution)/shard_map/all_to_all | solution.py:90
  135.7 2.8 collective-permute-start.1
  138.5 2.8 collective-permute-done.1
  141.3 2.9 collective-permute-start.2
  144.2 4.3 collective-permute-done.2
  148.5 0.3 reduce-window.36
  148.9 0.1 slice_reduce_fusion.2
  149.4 8.0 %scatter_custom_fusion = s32[1536]{0:T(1024)S(1)} fusion(s32[2048]{0:T(1024)S(1)} %bitcast.90, s32[2048]{0:T(1024)S(1)} %iota.29, s32[]{:T(128)} %constant.118.clone.1), kind=kCustom, calls=%fused_computation.119 | custom fusion | bytes 6148 | tf_op jit(solution)/shard_map/scatter | solution.py:48
  157.4 0.1 broadcast_in_dim.74
  157.5 0.1 broadcast_in_dim.76
  157.7 9.0 %gather_fusion = bf16[1536,768]{1,0:T(8,128)(2,1)} fusion(bf16[2048,768]{1,0:T(8,128)(2,1)} %all-gather.2.cloned.1.call-done, s32[2048]{0:T(1024)S(1)} %pad_clamp_fusion), kind=kCustom, calls=%fused_computation | custom fusion | bytes 4724736 | tf_op jit(solution)/shard_map/jit(_take)/gather | solution.py:120
  166.7 3.0 select_select_fusion.1
  169.7 29.7 %while.11 = (s32[]{:T(128)}, bf16[8,192,768]{2,1,0:T(8,128)(2,1)S(1)}, bf16[8,192,768]{2,1,0:T(8,128)(2,1)}, bf16[768,1536]{1,0:T(8,128)(2,1)}, bf16[1536,768]{1,0:T(8,128)(2,1)}) while((s32[]{:T(128)}, bf16[8,192,768]{2,1,0:T(8,128)(2,1)S(1)}, bf16[8,192,768]{2,1,0:T(8,128)(2,1)}, bf16[768,1536]{1,0:T(8,128)(2,1)}, ...), condition=%wide.region_12.13_spmd.clone, body=%wide.region_11.12_spmd.sunk.clone | while | flops 906706944 | bytes 5309509 | solution.py:41
  169.7 3.7 fusion.84
  173.4 3.7 fusion.84
  177.1 3.7 fusion.84
  180.8 3.7 fusion.84
  184.6 3.7 fusion.84
  188.3 3.7 fusion.84
  192.0 3.7 fusion.84
  195.7 3.7 fusion.84
  199.4 9.4 %gather_fusion.1 = bf16[2048,768]{1,0:T(8,128)(2,1)} fusion(bf16[1536,768]{1,0:T(8,128)(2,1)S(1)} %bitcast.82, s32[2048]{0:T(1024)S(1)} %broadcast_clamp_fusion), kind=kCustom, calls=%fused_computation.1 | custom fusion | bytes 6299648 | tf_op jit(solution)/shard_map/jit(_take)/gather | solution.py:125
  208.8 3.5 select_select_fusion
  212.2 3.8 all-to-all-start.3
  216.1 0.1 reshape.297
  216.2 0.1 gt.37
  216.3 0.1 copy.46
  216.5 0.1 sub.43
  216.7 0.2 fusion.11
  216.9 37.3 %all-to-all-done.3 = bf16[8,256,768]{2,1,0:T(8,128)(2,1)S(1)} async-done(((bf16[8,256,768]{2,1,0:T(8,128)(2,1)}), bf16[8,256,768]{2,1,0:T(8,128)(2,1)S(1)}, u32[]{:S(2)}, u32[]{:S(2)}) %all-to-all-start.3) | async-done | bytes 3145760 | tf_op jit(solution)/shard_map/all_to_all | solution.py:127
  254.3 0.6 multiply_reduce_fusion
  254.9 2.2 fusion.12
  257.1 1.4 copy.51
  258.6 158.5 %all_to_all.25 = f32[64,12,768]{2,1,0:T(8,128)S(1)} all-to-all(f32[64,12,768]{2,1,0:T(8,128)S(1)} %copy.51), channel_id=1, replica_groups=mesh['grp'=64,'dev'=8] {'grp'}, dimensions={0} | all-to-all | bytes 4718592 | tf_op jit(solution)/shard_map/all_to_all | solution.py:138
  417.1 1.5 reshape.306
  418.7 3.9 convolution_convert_fusion.3
  (53 shorter events, 1.3 us)
Async XLA Ops:
  6.5 22.8 %copy-start = (bf16[64,768]{1,0:T(8,128)(2,1)S(1)}, bf16[64,768]{1,0:T(8,128)(2,1)}, u32[]{:S(2)}) copy-start(bf16[64,768]{1,0:T(8,128)(2,1)} %param.7) | copy-start | bytes 294916
  10.0 31.7 %all-to-all-start = ((s32[64,12,2]{1,2,0:T(2,128)}), s32[64,12,2]{1,2,0:T(2,128)S(1)}, u32[]{:S(2)}, u32[]{:S(2)}) async-start(s32[64,12,2]{1,2,0:T(2,128)} %copy.43), calls=%async_computation | async-start | bytes 131072 | tf_op jit(solution)/shard_map/all_to_all | solution.py:87
  41.7 81.5 %all-to-all-start.2 = ((bf16[64,12,768]{2,1,0:T(8,128)(2,1)}), bf16[64,12,768]{2,1,0:T(8,128)(2,1)S(1)}, u32[]{:S(2)}, u32[]{:S(2)}) async-start(bf16[64,12,768]{2,1,0:T(8,128)(2,1)} %reshape.303), calls=%async_computation.2 | async-start | bytes 3145728 | tf_op jit(solution)/shard_map/all_to_all | solution.py:80
  48.2 109.6 %all-gather.2.cloned.1.call-start = ((), (), s32[]{:S(2)}) async-start(), calls=%async_computation.5 | async-start | bytes 3538944 | tf_op jit(solution)/shard_map/all_gather | solution.py:111
  48.9 75.8 %copy-start.1 = (bf16[64,8]{0,1:T(8,128)(2,1)S(1)}, bf16[64,8]{0,1:T(8,128)(2,1)}, u32[]{:S(2)}) copy-start(bf16[64,8]{0,1:T(8,128)(2,1)} %param.9) | copy-start | bytes 3076
  125.5 10.1 %collective-permute-start = (s32[256,2]{0,1:T(2,128)S(1)}, s32[256,2]{0,1:T(2,128)S(1)}, u32[]{:S(2)}, u32[]{:S(2)}) collective-permute-start(s32[256,2]{0,1:T(2,128)S(1)} %get-tuple-element.50), channel_id=1, source_target_pairs={{0,7},{1,0},{2,1},{3,2},{4,3},{5,4},{6,5},{7,6},{8,15},{9,8},{10,9... | collective-permute-start | bytes 6152 | tf_op jit(solution)/shard_map/ppermute | solution.py:12
  126.6 85.7 %all-to-all-start.1 = ((bf16[64,12,2]{1,2,0:T(2,128)(2,1)}), bf16[64,12,2]{1,2,0:T(2,128)(2,1)S(1)}, u32[]{:S(2)}, u32[]{:S(2)}) async-start(bf16[64,12,2]{1,2,0:T(2,128)(2,1)} %copy.48), calls=%async_computation.1 | async-start | bytes 65536 | tf_op jit(solution)/shard_map/all_to_all | solution.py:90
  135.7 5.6 %collective-permute-start.1 = (s32[512,2]{0,1:T(2,128)S(1)}, s32[512,2]{0,1:T(2,128)S(1)}, u32[]{:S(2)}, u32[]{:S(2)}) collective-permute-start(s32[512,2]{0,1:T(2,128)S(1)} %pad_add_fusion.1), channel_id=1, source_target_pairs={{0,6},{1,7},{2,0},{3,1},{4,2},{5,3},{6,4},{7,5},{8,14},{9,15},{10,... | collective-permute-start | bytes 12296 | tf_op jit(solution)/shard_map/ppermute | solution.py:12
  141.3 7.2 %collective-permute-start.2 = (s32[1024,2]{0,1:T(2,128)S(1)}, s32[1024,2]{0,1:T(2,128)S(1)}, u32[]{:S(2)}, u32[]{:S(2)}) collective-permute-start(s32[1024,2]{0,1:T(2,128)S(1)} %pad_add_fusion), channel_id=1, source_target_pairs={{0,4},{1,5},{2,6},{3,7},{4,0},{5,1},{6,2},{7,3},{8,12},{9,13},{10,... | collective-permute-start | bytes 24584 | tf_op jit(solution)/shard_map/ppermute | solution.py:12
  212.2 42.0 %all-to-all-start.3 = ((bf16[8,256,768]{2,1,0:T(8,128)(2,1)}), bf16[8,256,768]{2,1,0:T(8,128)(2,1)S(1)}, u32[]{:S(2)}, u32[]{:S(2)}) async-start(bf16[8,256,768]{2,1,0:T(8,128)(2,1)} %select_select_fusion), calls=%async_computation.3 | async-start | bytes 6291456 | tf_op jit(solution)/shard_map/all_to_all | solution.py:127
Sparse Core Ops, SparseCore 0:
  124.9 28.1 all-gather.1
